TPU v7x, 32 devices: a whole 2x2x4 slice. The times are simulated.
32 devices in a mesh: row: 4 (over z), col: 8 (over y, x, core).
Axes of the slice: x: 2, y: 2, z: 4, core: 2. Of those that a mesh axis runs over, the one named last changes fastest.
Arguments:
- item_table: float32 [1310720, 128], P(('row', 'col')), may hold values from -6 to 6
- owner_ids: int32 [4096, 50], P(('row', 'col')), may hold values from 0 to 31, as said below
- row_ids: int32 [4096, 50], P(('row', 'col')), may hold values from 0 to 40959
- lengths: int32 [4096], P(('row', 'col')), may hold values from 25 to 50
- dense_input: bfloat16 [4096, 256], P(('row', 'col')), may hold values from -6 to 6
- w_bottom: bfloat16 [256, 256], replicated, may hold values from -0.375 to 0.375
Outputs:
- features: float32 [4096, 384], P(('row', 'col'))
Inputs may be any that keep to these rules, and one draw needn't show every extreme that they name: Among the live positions (p < lengths[u]) of the 128 users of one device, at most 300 have the same owner_ids value; in every draw some owner_ids values receive exactly 300 live positions from every device.
All inputs are finite; a program needn't handle non-finite values.
Results may differ from a plain program's by a relative error of at most 0.0003.
Values sent between devices are 32-bit elements; how exact they have to be, the bound alone decides.
A program may use at most 128 MiB of HBM per device.

v0:
```python
import functools

import jax
import jax.numpy as jnp
from jax import lax
from jax.experimental import pallas as pl
from jax.experimental.pallas import tpu as pltpu
from jax.sharding import PartitionSpec as P

MESH = pl.DeviceIdType.MESH
LANES = 128
SUBLANES = 8


def round_up(value, unit):
    return -(-value // unit) * unit


def drain(ref, sem):
    pltpu.make_async_copy(ref, ref, sem).wait()


def kernel(
    sizes,
    table_hbm, owner_hbm, row_hbm, len_hbm, dense_hbm, w_hbm, pooled_ref, silu_ref,
    owner_ref, row_ref, len_ref, dense_ref, w_ref,
    table, owner_live, acc, index_out, index_in, index_tile, index_smem, gather0, gather1,
    send_c, total, recv_c, recv_ax, recv_ay, recv_by, recv_bx, recv_z,
    owner_sem, row_sem, len_sem, dense_sem, w_sem,
    table_sem, index_send_sem, index_recv_sem, own_sem, smem_sem,
    send_c_sem, send_ax_sem, send_ay_sem, send_by_sem, send_bx_sem, send_z_sem,
    recv_c_sem, recv_ax_sem, recv_ay_sem, recv_by_sem, recv_bx_sem, recv_z_sem,
):
    nz, ncol, ny, nx, nc, cap = sizes
    owners = nz * ncol
    hist, users = owner_ref.shape
    half = users // 2
    width = acc.shape[0]
    tiles = width // LANES
    cap_rows = round_up(cap, 16)
    z = lax.axis_index("row")
    col = lax.axis_index("col")
    me = z * ncol + col
    c = col % nc
    x = (col // nc) % nx
    y = col // (nc * nx)

    def column(y_at, x_at, c_at):
        return (y_at * nx + x_at) * nc + c_at

    small = [
        pltpu.make_async_copy(*refs)
        for refs in (
            (len_hbm, len_ref, len_sem), (owner_hbm, owner_ref, owner_sem),
            (row_hbm, row_ref, row_sem), (dense_hbm, dense_ref, dense_sem),
            (w_hbm, w_ref, w_sem),
        )
    ]
    for copy in small:
        copy.start()

    pieces = 8
    piece = table.shape[0] // pieces
    for at in range(pieces):
        rows = pl.ds(at * piece, piece)
        pltpu.make_async_copy(table_hbm.at[rows], table.at[rows], table_sem).start()

    barrier = pltpu.get_barrier_semaphore()

    @pl.loop(1, owners)
    def _(step):
        there = lax.rem(me + step, owners)
        pl.semaphore_signal(
            barrier, inc=1, device_id=(there // ncol, lax.rem(there, ncol)), device_id_type=MESH
        )

    for copy in small[:3]:
        copy.wait()
    lengths = len_ref[...]
    position = lax.broadcasted_iota(jnp.int32, (hist, users), 0)
    owner_live[...] = jnp.where(position < lengths, owner_ref[...], -1)
    owner_iota = lax.broadcasted_iota(jnp.int32, (owners, users), 0)

    def count(at, carry):
        return carry + jnp.where(owner_live[pl.ds(at, 1), :] == owner_iota, 1.0, 0.0)

    per_user = lax.fori_loop(0, hist, count, jnp.zeros((owners, users), jnp.float32), unroll=5)
    before = lax.broadcasted_iota(jnp.int32, (users, users), 0) < lax.broadcasted_iota(
        jnp.int32, (users, users), 1
    )
    offsets = jnp.dot(
        per_user.astype(jnp.bfloat16),
        jnp.where(before, 1.0, 0.0).astype(jnp.bfloat16),
        preferred_element_type=jnp.float32,
    )
    acc[...] = jnp.zeros_like(acc)
    slot_iota = lax.broadcasted_iota(jnp.int32, (cap_rows, users), 0).astype(jnp.float32)
    user_number = lax.broadcasted_iota(jnp.int32, (1, users), 1).astype(jnp.float32) + 1.0
    group = 5 if hist % 5 == 0 else 1

    def place(step, counts):
        left, right = [], []
        for k in range(group):
            at = step * group + k
            row_id = row_ref[pl.ds(at, 1), :]
            high = row_id // 256
            low = (row_id - high * 256).astype(jnp.float32)
            high = high.astype(jnp.float32)
            match = owner_live[pl.ds(at, 1), :] == owner_iota
            rank = jnp.sum(jnp.where(match, counts, 0.0), axis=0, keepdims=True)
            counts = counts + jnp.where(match, 1.0, 0.0)
            right.append(jnp.where(slot_iota == rank, 1.0, 0.0).astype(jnp.bfloat16))
            values = [jnp.where(match, v, 0.0) for v in (high, low, user_number)]
            left.append(jnp.concatenate(values, axis=0).astype(jnp.bfloat16))
        acc[:cap_rows, :3 * owners] += lax.dot_general(
            jnp.concatenate(right, axis=1),
            jnp.concatenate(left, axis=1),
            (((1,), (1,)), ((), ())),
            preferred_element_type=jnp.float32,
        )
        return counts

    lax.fori_loop(0, hist // group, place, offsets)
    for at in range(tiles):
        found = acc[at * LANES:(at + 1) * LANES, :].T
        rows = found[0:owners] * 256.0 + found[owners:2 * owners]
        index_out[:, at, :] = rows.astype(jnp.int32)
        index_out[:, tiles + at, :] = found[2 * owners:3 * owners].astype(jnp.int32)

    pl.semaphore_wait(barrier, owners - 1)

    @pl.loop(1, owners)
    def _(step):
        there = lax.rem(me + step, owners)
        pltpu.make_async_remote_copy(
            src_ref=index_out.at[there],
            dst_ref=index_in.at[me],
            send_sem=index_send_sem,
            recv_sem=index_recv_sem,
            device_id=(there // ncol, lax.rem(there, ncol)),
            device_id_type=MESH,
        ).start()

    own = pltpu.make_async_copy(index_out.at[me], index_in.at[me], own_sem)
    own.start()

    for copy in small[3:]:
        copy.wait()
    hidden = jnp.dot(dense_ref[...], w_ref[...], preferred_element_type=jnp.float32)
    dim = pooled_ref.shape[1]
    silu_ref[...] = hidden / (1.0 + jnp.exp(-hidden))
    gather0[...] = jnp.zeros_like(gather0)
    gather1[...] = jnp.zeros_like(gather1)

    own.wait()
    drain(index_in.at[pl.ds(0, owners - 1)], index_recv_sem)
    row_ids = index_in[:, :tiles, :]
    lane_iota = lax.broadcasted_iota(jnp.int32, row_ids.shape, 2)
    index_tile[:, :tiles, :] = jnp.clip(row_ids >> 3, 0, table.shape[0] - 1)
    index_tile[:, tiles:2 * tiles, :] = (lane_iota - row_ids) & (SUBLANES - 1)
    to_smem = pltpu.make_async_copy(index_tile, index_smem, smem_sem)
    to_smem.start()
    to_smem.wait()
    drain(table, table_sem)

    user_iota = lax.broadcasted_iota(jnp.int32, (users, LANES), 0) + 1

    sublane = lax.broadcasted_iota(jnp.int32, (SUBLANES, dim), 0)

    def fetch(source, gathered):
        for first in range(0, cap_rows, SUBLANES):
            rows = None
            for k in range(SUBLANES):
                tile_at, lane = divmod(first + k, LANES)
                tile = table[index_smem[source, tile_at, lane]]
                moved = pltpu.roll(tile, index_smem[source, tiles + tile_at, lane], 0)
                rows = moved if k == 0 else jnp.where(sublane == k, moved, rows)
            gathered[first:first + SUBLANES, :] = rows

    def block_sum(source, gathered):
        names = [index_in[source, pl.ds(tiles + at, 1), :] for at in range(tiles)]
        select = jnp.concatenate(
            [jnp.where(name == user_iota, 1.0, 0.0).astype(jnp.bfloat16) for name in names], axis=1
        )
        values = gathered[...]
        high = values.astype(jnp.bfloat16)
        low = (values - high.astype(jnp.float32)).astype(jnp.bfloat16)
        both = jnp.dot(
            select, jnp.concatenate([high, low], axis=1), preferred_element_type=jnp.float32
        )
        return both[:, :dim] + both[:, dim:]

    def send(src, dst, send_sem, recv_sem, z_at, col_at):
        pltpu.make_async_remote_copy(
            src_ref=src, dst_ref=dst, send_sem=send_sem, recv_sem=recv_sem,
            device_id=(z_at, col_at), device_id_type=MESH,
        ).start()

    def source_of(dx, dy, dz):
        return lax.rem(z + dz, nz) * ncol + column(lax.rem(y + dy, ny), lax.rem(x + dx, nx), 0)

    def offsets_at(step):
        group = step // nz
        return nx - 1 - group % nx, ny - 1 - group // nx, (step + 1) % nz

    def handle(step, last):
        dx, dy, dz = offsets_at(step)
        yt, xt = lax.rem(y + dy, ny), lax.rem(x + dx, nx)
        slot = (dy * nx + dx) * nz + dz
        base = source_of(dx, dy, dz)
        send_c[slot] = block_sum(base + 1 - c, gather0)
        fetch(base + c, gather1)
        send(send_c.at[slot], recv_c.at[slot], send_c_sem, recv_c_sem.at[slot],
             z, column(y, x, 1 - c))
        total[slot] = block_sum(base + c, gather1)
        if not last:
            fetch(source_of(*offsets_at(step + 1)) + 1 - c, gather0)
        drain(recv_c.at[slot], recv_c_sem.at[slot])
        total[slot] += recv_c[slot]
        near_x, near_y = dx == 0, dy == 0
        both = jnp.logical_and(near_x, near_y)
        upper, lower = pl.ds(0, half), pl.ds(half, half)

        def add(part, landed, sem, at):
            drain(landed.at[at], sem.at[at])
            total[slot, part] += landed[at]

        @pl.when(near_x)
        def _():
            for k in range(nx - 1):
                add(upper, recv_ax, recv_ax_sem, (k * ny + dy) * nz + dz)

        @pl.when(near_y)
        def _():
            for k in range(ny - 1):
                add(lower, recv_by, recv_by_sem, (k * nx + dx) * nz + dz)

        @pl.when(both)
        def _():
            for k in range(ny - 1):
                add(upper, recv_ay, recv_ay_sem, k * nz + dz)
            for k in range(nx - 1):
                add(lower, recv_bx, recv_bx_sem, k * nz + dz)

        @pl.when(dx > 0)
        def _():
            at = ((dx - 1) * ny + dy) * nz + dz
            send(total.at[slot, upper], recv_ax.at[at], send_ax_sem, recv_ax_sem.at[at],
                 z, column(y, xt, c))

        @pl.when(dy > 0)
        def _():
            at = ((dy - 1) * nx + dx) * nz + dz
            send(total.at[slot, lower], recv_by.at[at], send_by_sem, recv_by_sem.at[at],
                 z, column(yt, x, c))

        @pl.when(jnp.logical_and(near_x, dy > 0))
        def _():
            at = (dy - 1) * nz + dz
            send(total.at[slot, upper], recv_ay.at[at], send_ay_sem, recv_ay_sem.at[at],
                 z, column(yt, x, c))

        @pl.when(jnp.logical_and(near_y, dx > 0))
        def _():
            at = (dx - 1) * nz + dz
            send(total.at[slot, lower], recv_bx.at[at], send_bx_sem, recv_bx_sem.at[at],
                 z, column(y, xt, c))

        @pl.when(jnp.logical_and(both, dz > 0))
        def _():
            send(total.at[dz], recv_z.at[dz - 1], send_z_sem, recv_z_sem.at[dz - 1],
                 lax.rem(z + dz, nz), col)

    chips = nz * ny * nx
    fetch(source_of(*offsets_at(0)) + 1 - c, gather0)

    @pl.loop(0, chips - 1)
    def _(step):
        handle(step, False)

    handle(jnp.int32(chips - 1), True)
    pooled = total[0]
    for k in range(nz - 1):
        drain(recv_z.at[k], recv_z_sem.at[k])
        pooled = pooled + recv_z[k]
    divisor = jnp.broadcast_to(lengths.astype(jnp.float32), (users, users)).T
    pooled_ref[...] = pooled / divisor[:, :1]

    drain(index_in.at[pl.ds(0, owners - 1)], index_send_sem)
    drain(send_c, send_c_sem)
    drain(recv_ax, send_ax_sem)
    drain(recv_ay, send_ay_sem)
    drain(recv_by, send_by_sem)
    drain(recv_bx, send_bx_sem)
    drain(recv_z, send_z_sem)


def per_device(nz, ncol, item_table, owner_ids, row_ids, lengths, dense_input, w_bottom):
    users, hist = owner_ids.shape
    rows, dim = item_table.shape
    owners = nz * ncol
    cap = 3 * users * hist // (2 * owners)
    width = round_up(cap, LANES)
    tile_rows = round_up(2 * (width // LANES), SUBLANES)
    nc, nx = 2, 2
    ny = ncol // (nc * nx)
    chips = nz * ny * nx
    half = users // 2
    ax, ay, by, bx = (nx - 1) * ny * nz, (ny - 1) * nz, (ny - 1) * nx * nz, (nx - 1) * nz
    dma = pltpu.SemaphoreType.DMA
    vmem = pl.BlockSpec(memory_space=pltpu.VMEM)

    def floats(*shape):
        return pltpu.VMEM(shape, jnp.float32)

    pooled, dense_out = pl.pallas_call(
        functools.partial(kernel, (nz, ncol, ny, nx, nc, cap)),
        out_shape=[
            jax.ShapeDtypeStruct((users, dim), jnp.float32),
            jax.ShapeDtypeStruct((users, w_bottom.shape[1]), jnp.float32),
        ],
        in_specs=[pl.BlockSpec(memory_space=pl.ANY)] * 6,
        out_specs=[vmem, vmem],
        scratch_shapes=[
            pltpu.VMEM((hist, users), jnp.int32),
            pltpu.VMEM((hist, users), jnp.int32),
            pltpu.VMEM((1, users), jnp.int32),
            pltpu.VMEM(dense_input.shape, dense_input.dtype),
            pltpu.VMEM(w_bottom.shape, w_bottom.dtype),
            floats(rows // SUBLANES, SUBLANES, dim),
            pltpu.VMEM((hist, users), jnp.int32),
            floats(width, round_up(3 * owners, LANES)),
            pltpu.VMEM((owners, tile_rows, LANES), jnp.int32),
            pltpu.VMEM((owners, tile_rows, LANES), jnp.int32),
            pltpu.VMEM((owners, tile_rows, LANES), jnp.int32),
            pltpu.SMEM((owners, tile_rows, LANES), jnp.int32),
            floats(width, dim),
            floats(width, dim),
            floats(chips, users, dim),
            floats(chips, users, dim),
            floats(chips, users, dim),
            floats(ax, half, dim),
            floats(ay, half, dim),
            floats(by, half, dim),
            floats(bx, half, dim),
            floats(nz - 1, users, dim),
        ]
        + [dma] * 16
        + [dma((chips,)), dma((ax,)), dma((ay,)), dma((by,)), dma((bx,)), dma((nz - 1,))],
        compiler_params=pltpu.CompilerParams(
            collective_id=0, has_side_effects=True, vmem_limit_bytes=56 * 1024 * 1024
        ),
    )(item_table.reshape(rows // SUBLANES, SUBLANES, dim), owner_ids.T, row_ids.T, lengths[None, :], dense_input, w_bottom)
    return jnp.concatenate([pooled, dense_out], axis=1)


def solution(mesh):
    in_specs = (
        P(("row", "col"), None),
        P(("row", "col"), None),
        P(("row", "col"), None),
        P(("row", "col")),
        P(("row", "col"), None),
        P(),
    )
    out_specs = P(("row", "col"), None)
    body = functools.partial(per_device, mesh.shape["row"], mesh.shape["col"])
    return jax.shard_map(
        body, mesh=mesh, in_specs=in_specs, out_specs=out_specs, check_vma=False
    )
```

profile of v0, /device:TPU:0, one launch (start us, length us, event | category | flops | bytes accessed | tf_op | source)
XLA Modules:
  0.0 57.2 jit_solution(17871862731947077383)
XLA Ops:
  0.0 55.6 %shard_map.64 = (f32[128,128]{1,0:T(8,128)}, f32[128,256]{1,0:T(8,128)}) custom-call(f32[5120,8,128]{2,1,0:T(8,128)} %bitcast.4, s32[50,128]{1,0:T(8,128)} %bitcast.5, s32[50,128]{1,0:T(8,128)} %bitcast.6, s32[1,128]{1,0:T(1,128)} %bitcast.7, bf16[128,256]{1,0:T(8,128)(2,1)} %dense_hbm.1, bf16[256,256]{1,0:T(8,128)(2,1)} %w_hbm.1), custom_call_target="tpu_custom_call" | custom-call | tf_op jit(solution)/shard_map/pallas_call | solution.py:316
  55.6 1.6 %pad_maximum_fusion = f32[128,384]{1,0:T(8,128)} fusion(f32[128,256]{1,0:T(8,128)} %get-tuple-element.8, f32[128,128]{1,0:T(8,128)} %get-tuple-element.7), kind=kLoop, calls=%fused_computation | loop fusion | flops 49152 | bytes 393216 | tf_op jit(solution)/shard_map/concatenate | solution.py:354
where the time goes:
time: 57.4 us; the launch traced here: 57.2 us
  Pallas kernels  55.6 us (97%)
  other arithmetic  1.6 us (3%)
    pallas_call x1, Pallas kernels, per_device(): pl.pallas_call(functools.partial(kernel, (nz, ncol, ny, nx, nc, cap)), ou...  55.6 us
    concatenate x1, other arithmetic, per_device(): return jnp.concatenate([pooled, dense_out], axis=1)  1.6 us

commit v1 on v0

--- a/solution.py
+++ b/solution.py
@@ -24,7 +24,7 @@
     sizes,
     table_hbm, owner_hbm, row_hbm, len_hbm, dense_hbm, w_hbm, pooled_ref, silu_ref,
     owner_ref, row_ref, len_ref, dense_ref, w_ref,
-    table, owner_live, acc, index_out, index_in, index_tile, index_smem, gather0, gather1,
+    table, owner_live, acc, index_out, index_in, index_smem, gather0, gather1,
     send_c, total, recv_c, recv_ax, recv_ay, recv_by, recv_bx, recv_z,
     owner_sem, row_sem, len_sem, dense_sem, w_sem,
     table_sem, index_send_sem, index_recv_sem, own_sem, smem_sem,
@@ -124,7 +124,7 @@
     for at in range(tiles):
         found = acc[at * LANES:(at + 1) * LANES, :].T
         rows = found[0:owners] * 256.0 + found[owners:2 * owners]
-        index_out[:, at, :] = rows.astype(jnp.int32)
+        index_out[:, at, :] = jnp.clip(rows.astype(jnp.int32), 0, table.shape[0] - 1)
         index_out[:, tiles + at, :] = found[2 * owners:3 * owners].astype(jnp.int32)
 
     pl.semaphore_wait(barrier, owners - 1)
@@ -154,28 +154,17 @@
 
     own.wait()
     drain(index_in.at[pl.ds(0, owners - 1)], index_recv_sem)
-    row_ids = index_in[:, :tiles, :]
-    lane_iota = lax.broadcasted_iota(jnp.int32, row_ids.shape, 2)
-    index_tile[:, :tiles, :] = jnp.clip(row_ids >> 3, 0, table.shape[0] - 1)
-    index_tile[:, tiles:2 * tiles, :] = (lane_iota - row_ids) & (SUBLANES - 1)
-    to_smem = pltpu.make_async_copy(index_tile, index_smem, smem_sem)
+    to_smem = pltpu.make_async_copy(index_in, index_smem, smem_sem)
     to_smem.start()
     to_smem.wait()
     drain(table, table_sem)
 
     user_iota = lax.broadcasted_iota(jnp.int32, (users, LANES), 0) + 1
 
-    sublane = lax.broadcasted_iota(jnp.int32, (SUBLANES, dim), 0)
-
     def fetch(source, gathered):
-        for first in range(0, cap_rows, SUBLANES):
-            rows = None
-            for k in range(SUBLANES):
-                tile_at, lane = divmod(first + k, LANES)
-                tile = table[index_smem[source, tile_at, lane]]
-                moved = pltpu.roll(tile, index_smem[source, tiles + tile_at, lane], 0)
-                rows = moved if k == 0 else jnp.where(sublane == k, moved, rows)
-            gathered[first:first + SUBLANES, :] = rows
+        for slot in range(cap):
+            row = index_smem[source, slot // LANES, slot % LANES]
+            gathered[slot:slot + 1, :] = table[pl.ds(row, 1), :]
 
     def block_sum(source, gathered):
         names = [index_in[source, pl.ds(tiles + at, 1), :] for at in range(tiles)]
@@ -203,9 +192,8 @@
         group = step // nz
         return nx - 1 - group % nx, ny - 1 - group // nx, (step + 1) % nz
 
-    def handle(step, last):
+    def compute(step):
         dx, dy, dz = offsets_at(step)
-        yt, xt = lax.rem(y + dy, ny), lax.rem(x + dx, nx)
         slot = (dy * nx + dx) * nz + dz
         base = source_of(dx, dy, dz)
         send_c[slot] = block_sum(base + 1 - c, gather0)
@@ -213,8 +201,12 @@
         send(send_c.at[slot], recv_c.at[slot], send_c_sem, recv_c_sem.at[slot],
              z, column(y, x, 1 - c))
         total[slot] = block_sum(base + c, gather1)
-        if not last:
-            fetch(source_of(*offsets_at(step + 1)) + 1 - c, gather0)
+        fetch(source_of(*offsets_at((step + 1) % chips)) + 1 - c, gather0)
+
+    def combine(step):
+        dx, dy, dz = offsets_at(step)
+        yt, xt = lax.rem(y + dy, ny), lax.rem(x + dx, nx)
+        slot = (dy * nx + dx) * nz + dz
         drain(recv_c.at[slot], recv_c_sem.at[slot])
         total[slot] += recv_c[slot]
         near_x, near_y = dx == 0, dy == 0
@@ -274,11 +266,18 @@
     chips = nz * ny * nx
     fetch(source_of(*offsets_at(0)) + 1 - c, gather0)
 
-    @pl.loop(0, chips - 1)
+    delay = min(3, chips)
+
+    @pl.loop(0, chips + delay)
     def _(step):
-        handle(step, False)
-
-    handle(jnp.int32(chips - 1), True)
+        @pl.when(step < chips)
+        def _():
+            compute(step)
+
+        @pl.when(step >= delay)
+        def _():
+            combine(step - delay)
+
     pooled = total[0]
     for k in range(nz - 1):
         drain(recv_z.at[k], recv_z_sem.at[k])
@@ -327,10 +326,9 @@
             pltpu.VMEM((1, users), jnp.int32),
             pltpu.VMEM(dense_input.shape, dense_input.dtype),
             pltpu.VMEM(w_bottom.shape, w_bottom.dtype),
-            floats(rows // SUBLANES, SUBLANES, dim),
+            floats(rows, dim),
             pltpu.VMEM((hist, users), jnp.int32),
             floats(width, round_up(3 * owners, LANES)),
-            pltpu.VMEM((owners, tile_rows, LANES), jnp.int32),
             pltpu.VMEM((owners, tile_rows, LANES), jnp.int32),
             pltpu.VMEM((owners, tile_rows, LANES), jnp.int32),
             pltpu.SMEM((owners, tile_rows, LANES), jnp.int32),
@@ -350,7 +348,7 @@
         compiler_params=pltpu.CompilerParams(
             collective_id=0, has_side_effects=True, vmem_limit_bytes=56 * 1024 * 1024
         ),
-    )(item_table.reshape(rows // SUBLANES, SUBLANES, dim), owner_ids.T, row_ids.T, lengths[None, :], dense_input, w_bottom)
+    )(item_table, owner_ids.T, row_ids.T, lengths[None, :], dense_input, w_bottom)
     return jnp.concatenate([pooled, dense_out], axis=1)
 
 

time: 57.4 us -> 43.1 us (0.75)
  Pallas kernels: 55.6 us -> 41.4 us
    pallas_call x1, Pallas kernels: 55.6 us -> 41.4 us  [per_device(): pl.pallas_call(functools.partial(kernel, (nz, ncol, ny, nx, nc, cap)), ou...]
where the time goes in v1:
time: 43.1 us; the launch traced here: 43 us
  Pallas kernels  41.4 us (96%)
  other arithmetic  1.6 us (4%)
    pallas_call x1, Pallas kernels, per_device(): pl.pallas_call(functools.partial(kernel, (nz, ncol, ny, nx, nc, cap)), ou...  41.4 us
    concatenate x1, other arithmetic, per_device(): return jnp.concatenate([pooled, dense_out], axis=1)  1.6 us

profile of v1, /device:TPU:0, one launch (start us, length us, event | category | flops | bytes accessed | tf_op | source)
XLA Modules:
  0.0 43.0 jit_solution(9259150561301261289)
XLA Ops:
  0.0 41.4 %shard_map.64 = (f32[128,128]{1,0:T(8,128)}, f32[128,256]{1,0:T(8,128)}) custom-call(f32[40960,128]{1,0:T(8,128)} %table_hbm.1, s32[50,128]{1,0:T(8,128)} %bitcast.3, s32[50,128]{1,0:T(8,128)} %bitcast.4, s32[1,128]{1,0:T(1,128)} %bitcast.5, bf16[128,256]{1,0:T(8,128)(2,1)} %dense_hbm.1, bf16[256,256]{1,0:T(8,128)(2,1)} %w_hbm.1), custom_call_target="tpu_custom_call" | custom-call | tf_op jit(solution)/shard_map/pallas_call | solution.py:315
  41.4 1.6 %pad_maximum_fusion = f32[128,384]{1,0:T(8,128)} fusion(f32[128,256]{1,0:T(8,128)} %get-tuple-element.8, f32[128,128]{1,0:T(8,128)} %get-tuple-element.7), kind=kLoop, calls=%fused_computation | loop fusion | flops 49152 | bytes 393216 | tf_op jit(solution)/shard_map/concatenate | solution.py:352

commit v2 on v1

--- a/solution.py
+++ b/solution.py
@@ -27,8 +27,8 @@
     table, owner_live, acc, index_out, index_in, index_smem, gather0, gather1,
     send_c, total, recv_c, recv_ax, recv_ay, recv_by, recv_bx, recv_z,
     owner_sem, row_sem, len_sem, dense_sem, w_sem,
-    table_sem, index_send_sem, index_recv_sem, own_sem, smem_sem,
-    send_c_sem, send_ax_sem, send_ay_sem, send_by_sem, send_bx_sem, send_z_sem,
+    table_sem, index_send_sem, index_recv_sem, own_sem,
+    send_c_sem, send_ax_sem, send_ay_sem, send_by_sem, send_bx_sem, send_z_sem, smem_sem,
     recv_c_sem, recv_ax_sem, recv_ay_sem, recv_by_sem, recv_bx_sem, recv_z_sem,
 ):
     nz, ncol, ny, nx, nc, cap = sizes
@@ -154,9 +154,26 @@
 
     own.wait()
     drain(index_in.at[pl.ds(0, owners - 1)], index_recv_sem)
-    to_smem = pltpu.make_async_copy(index_in, index_smem, smem_sem)
-    to_smem.start()
-    to_smem.wait()
+    chips = nz * ny * nx
+
+    def offsets_at(step):
+        group = step % (nx * ny)
+        return nx - 1 - group % nx, ny - 1 - group // nx, (step // (nx * ny) + 1) % nz
+
+    def source_of(dx, dy, dz):
+        return lax.rem(z + dz, nz) * ncol + column(lax.rem(y + dy, ny), lax.rem(x + dx, nx), 0)
+
+    def to_smem(source):
+        return pltpu.make_async_copy(
+            index_in.at[source], index_smem.at[source], smem_sem.at[source]
+        )
+
+    @pl.loop(0, chips)
+    def _(step):
+        base = source_of(*offsets_at(step))
+        to_smem(base + 1 - c).start()
+        to_smem(base + c).start()
+
     drain(table, table_sem)
 
     user_iota = lax.broadcasted_iota(jnp.int32, (users, LANES), 0) + 1
@@ -185,98 +202,105 @@
             device_id=(z_at, col_at), device_id_type=MESH,
         ).start()
 
-    def source_of(dx, dy, dz):
-        return lax.rem(z + dz, nz) * ncol + column(lax.rem(y + dy, ny), lax.rem(x + dx, nx), 0)
-
-    def offsets_at(step):
-        group = step // nz
-        return nx - 1 - group % nx, ny - 1 - group // nx, (step + 1) % nz
-
     def compute(step):
         dx, dy, dz = offsets_at(step)
         slot = (dy * nx + dx) * nz + dz
         base = source_of(dx, dy, dz)
+        following = source_of(*offsets_at((step + 1) % chips))
+        to_smem(base + c).wait()
+
+        @pl.when(step + 1 < chips)
+        def _():
+            to_smem(following + 1 - c).wait()
+
         send_c[slot] = block_sum(base + 1 - c, gather0)
         fetch(base + c, gather1)
         send(send_c.at[slot], recv_c.at[slot], send_c_sem, recv_c_sem.at[slot],
              z, column(y, x, 1 - c))
         total[slot] = block_sum(base + c, gather1)
-        fetch(source_of(*offsets_at((step + 1) % chips)) + 1 - c, gather0)
-
-    def combine(step):
+        fetch(following + 1 - c, gather0)
+
+    upper, lower = pl.ds(0, half), pl.ds(half, half)
+
+    def add(slot, part, landed, sem, at):
+        drain(landed.at[at], sem.at[at])
+        total[slot, part] += landed[at]
+
+    def after_core(step):
         dx, dy, dz = offsets_at(step)
-        yt, xt = lax.rem(y + dy, ny), lax.rem(x + dx, nx)
         slot = (dy * nx + dx) * nz + dz
         drain(recv_c.at[slot], recv_c_sem.at[slot])
         total[slot] += recv_c[slot]
-        near_x, near_y = dx == 0, dy == 0
-        both = jnp.logical_and(near_x, near_y)
-        upper, lower = pl.ds(0, half), pl.ds(half, half)
-
-        def add(part, landed, sem, at):
-            drain(landed.at[at], sem.at[at])
-            total[slot, part] += landed[at]
-
-        @pl.when(near_x)
-        def _():
-            for k in range(nx - 1):
-                add(upper, recv_ax, recv_ax_sem, (k * ny + dy) * nz + dz)
-
-        @pl.when(near_y)
-        def _():
-            for k in range(ny - 1):
-                add(lower, recv_by, recv_by_sem, (k * nx + dx) * nz + dz)
-
-        @pl.when(both)
-        def _():
-            for k in range(ny - 1):
-                add(upper, recv_ay, recv_ay_sem, k * nz + dz)
-            for k in range(nx - 1):
-                add(lower, recv_bx, recv_bx_sem, k * nz + dz)
 
         @pl.when(dx > 0)
         def _():
             at = ((dx - 1) * ny + dy) * nz + dz
             send(total.at[slot, upper], recv_ax.at[at], send_ax_sem, recv_ax_sem.at[at],
-                 z, column(y, xt, c))
+                 z, column(y, lax.rem(x + dx, nx), c))
 
         @pl.when(dy > 0)
         def _():
             at = ((dy - 1) * nx + dx) * nz + dz
             send(total.at[slot, lower], recv_by.at[at], send_by_sem, recv_by_sem.at[at],
-                 z, column(yt, x, c))
-
-        @pl.when(jnp.logical_and(near_x, dy > 0))
+                 z, column(lax.rem(y + dy, ny), x, c))
+
+    def after_first(step):
+        dx, dy, dz = offsets_at(step)
+        slot = (dy * nx + dx) * nz + dz
+
+        @pl.when(dx == 0)
+        def _():
+            for k in range(nx - 1):
+                add(slot, upper, recv_ax, recv_ax_sem, (k * ny + dy) * nz + dz)
+
+        @pl.when(dy == 0)
+        def _():
+            for k in range(ny - 1):
+                add(slot, lower, recv_by, recv_by_sem, (k * nx + dx) * nz + dz)
+
+        @pl.when(jnp.logical_and(dx == 0, dy > 0))
         def _():
             at = (dy - 1) * nz + dz
             send(total.at[slot, upper], recv_ay.at[at], send_ay_sem, recv_ay_sem.at[at],
-                 z, column(yt, x, c))
-
-        @pl.when(jnp.logical_and(near_y, dx > 0))
+                 z, column(lax.rem(y + dy, ny), x, c))
+
+        @pl.when(jnp.logical_and(dy == 0, dx > 0))
         def _():
             at = (dx - 1) * nz + dz
             send(total.at[slot, lower], recv_bx.at[at], send_bx_sem, recv_bx_sem.at[at],
-                 z, column(y, xt, c))
-
-        @pl.when(jnp.logical_and(both, dz > 0))
-        def _():
-            send(total.at[dz], recv_z.at[dz - 1], send_z_sem, recv_z_sem.at[dz - 1],
-                 lax.rem(z + dz, nz), col)
-
-    chips = nz * ny * nx
-    fetch(source_of(*offsets_at(0)) + 1 - c, gather0)
-
-    delay = min(3, chips)
-
-    @pl.loop(0, chips + delay)
+                 z, column(y, lax.rem(x + dx, nx), c))
+
+    def after_second(step):
+        dx, dy, dz = offsets_at(step)
+
+        @pl.when(jnp.logical_and(dx == 0, dy == 0))
+        def _():
+            for k in range(ny - 1):
+                add(dz, upper, recv_ay, recv_ay_sem, k * nz + dz)
+            for k in range(nx - 1):
+                add(dz, lower, recv_bx, recv_bx_sem, k * nz + dz)
+
+            @pl.when(dz > 0)
+            def _():
+                send(total.at[dz], recv_z.at[dz - 1], send_z_sem, recv_z_sem.at[dz - 1],
+                     lax.rem(z + dz, nz), col)
+
+    first_source = source_of(*offsets_at(0)) + 1 - c
+    to_smem(first_source).wait()
+    fetch(first_source, gather0)
+    delays = (2, 4, 6)
+
+    @pl.loop(0, chips + delays[-1])
     def _(step):
         @pl.when(step < chips)
         def _():
             compute(step)
 
-        @pl.when(step >= delay)
-        def _():
-            combine(step - delay)
+        for delay, stage in zip(delays, (after_core, after_first, after_second)):
+
+            @pl.when(jnp.logical_and(step >= delay, step < chips + delay))
+            def _():
+                stage(step - delay)
 
     pooled = total[0]
     for k in range(nz - 1):
@@ -343,7 +367,7 @@
             floats(bx, half, dim),
             floats(nz - 1, users, dim),
         ]
-        + [dma] * 16
+        + [dma] * 15 + [dma((owners,))]
         + [dma((chips,)), dma((ax,)), dma((ay,)), dma((by,)), dma((bx,)), dma((nz - 1,))],
         compiler_params=pltpu.CompilerParams(
             collective_id=0, has_side_effects=True, vmem_limit_bytes=56 * 1024 * 1024

time: 43.1 us -> 44.1 us (1.023)
  Pallas kernels: 41.4 us -> 42.3 us
    pallas_call x1, Pallas kernels: 41.4 us -> 42.3 us  [per_device(): pl.pallas_call(functools.partial(kernel, (nz, ncol, ny, nx, nc, cap)), ou...]
where the time goes in v2:
time: 44.1 us; the launch traced here: 43.9 us
  Pallas kernels  42.3 us (96%)
  other arithmetic  1.6 us (4%)
    pallas_call x1, Pallas kernels, per_device(): pl.pallas_call(functools.partial(kernel, (nz, ncol, ny, nx, nc, cap)), ou...  42.3 us
    concatenate x1, other arithmetic, per_device(): return jnp.concatenate([pooled, dense_out], axis=1)  1.6 us

profile of v2, /device:TPU:0, one launch (start us, length us, event | category | flops | bytes accessed | tf_op | source)
XLA Modules:
  0.0 43.9 jit_solution(632344052486270800)
XLA Ops:
  0.0 42.3 %shard_map.64 = (f32[128,128]{1,0:T(8,128)}, f32[128,256]{1,0:T(8,128)}) custom-call(f32[40960,128]{1,0:T(8,128)} %table_hbm.1, s32[50,128]{1,0:T(8,128)} %bitcast.3, s32[50,128]{1,0:T(8,128)} %bitcast.4, s32[1,128]{1,0:T(1,128)} %bitcast.5, bf16[128,256]{1,0:T(8,128)(2,1)} %dense_hbm.1, bf16[256,256]{1,0:T(8,128)(2,1)} %w_hbm.1), custom_call_target="tpu_custom_call" | custom-call | tf_op jit(solution)/shard_map/pallas_call | solution.py:339
  42.3 1.6 %pad_maximum_fusion = f32[128,384]{1,0:T(8,128)} fusion(f32[128,256]{1,0:T(8,128)} %get-tuple-element.8, f32[128,128]{1,0:T(8,128)} %get-tuple-element.7), kind=kLoop, calls=%fused_computation | loop fusion | flops 49152 | bytes 393216 | tf_op jit(solution)/shard_map/concatenate | solution.py:376

commit v3 on v2

--- a/solution.py
+++ b/solution.py
@@ -14,6 +14,18 @@
 
 def round_up(value, unit):
     return -(-value // unit) * unit
+
+
+def quotient(value, unit):
+    if unit & (unit - 1) == 0:
+        return value >> (unit.bit_length() - 1)
+    return value // unit
+
+
+def remainder(value, unit):
+    if unit & (unit - 1) == 0:
+        return value & (unit - 1)
+    return value % unit
 
 
 def drain(ref, sem):
@@ -41,9 +53,9 @@
     z = lax.axis_index("row")
     col = lax.axis_index("col")
     me = z * ncol + col
-    c = col % nc
-    x = (col // nc) % nx
-    y = col // (nc * nx)
+    c = remainder(col, nc)
+    x = remainder(quotient(col, nc), nx)
+    y = quotient(col, nc * nx)
 
     def column(y_at, x_at, c_at):
         return (y_at * nx + x_at) * nc + c_at
@@ -59,7 +71,7 @@
     for copy in small:
         copy.start()
 
-    pieces = 8
+    pieces = 32
     piece = table.shape[0] // pieces
     for at in range(pieces):
         rows = pl.ds(at * piece, piece)
@@ -69,9 +81,9 @@
 
     @pl.loop(1, owners)
     def _(step):
-        there = lax.rem(me + step, owners)
+        there = remainder(me + step, owners)
         pl.semaphore_signal(
-            barrier, inc=1, device_id=(there // ncol, lax.rem(there, ncol)), device_id_type=MESH
+            barrier, inc=1, device_id=(quotient(there, ncol), remainder(there, ncol)), device_id_type=MESH
         )
 
     for copy in small[:3]:
@@ -103,8 +115,8 @@
         for k in range(group):
             at = step * group + k
             row_id = row_ref[pl.ds(at, 1), :]
-            high = row_id // 256
-            low = (row_id - high * 256).astype(jnp.float32)
+            high = row_id >> 8
+            low = (row_id & 255).astype(jnp.float32)
             high = high.astype(jnp.float32)
             match = owner_live[pl.ds(at, 1), :] == owner_iota
             rank = jnp.sum(jnp.where(match, counts, 0.0), axis=0, keepdims=True)
@@ -131,13 +143,13 @@
 
     @pl.loop(1, owners)
     def _(step):
-        there = lax.rem(me + step, owners)
+        there = remainder(me + step, owners)
         pltpu.make_async_remote_copy(
             src_ref=index_out.at[there],
             dst_ref=index_in.at[me],
             send_sem=index_send_sem,
             recv_sem=index_recv_sem,
-            device_id=(there // ncol, lax.rem(there, ncol)),
+            device_id=(quotient(there, ncol), remainder(there, ncol)),
             device_id_type=MESH,
         ).start()
 
@@ -157,11 +169,15 @@
     chips = nz * ny * nx
 
     def offsets_at(step):
-        group = step % (nx * ny)
-        return nx - 1 - group % nx, ny - 1 - group // nx, (step // (nx * ny) + 1) % nz
+        group = remainder(step, nx * ny)
+        return (
+            nx - 1 - remainder(group, nx),
+            ny - 1 - quotient(group, nx),
+            remainder(quotient(step, nx * ny) + 1, nz),
+        )
 
     def source_of(dx, dy, dz):
-        return lax.rem(z + dz, nz) * ncol + column(lax.rem(y + dy, ny), lax.rem(x + dx, nx), 0)
+        return remainder(z + dz, nz) * ncol + column(remainder(y + dy, ny), remainder(x + dx, nx), 0)
 
     def to_smem(source):
         return pltpu.make_async_copy(
@@ -206,7 +222,7 @@
         dx, dy, dz = offsets_at(step)
         slot = (dy * nx + dx) * nz + dz
         base = source_of(dx, dy, dz)
-        following = source_of(*offsets_at((step + 1) % chips))
+        following = source_of(*offsets_at(remainder(step + 1, chips)))
         to_smem(base + c).wait()
 
         @pl.when(step + 1 < chips)
@@ -236,13 +252,13 @@
         def _():
             at = ((dx - 1) * ny + dy) * nz + dz
             send(total.at[slot, upper], recv_ax.at[at], send_ax_sem, recv_ax_sem.at[at],
-                 z, column(y, lax.rem(x + dx, nx), c))
+                 z, column(y, remainder(x + dx, nx), c))
 
         @pl.when(dy > 0)
         def _():
             at = ((dy - 1) * nx + dx) * nz + dz
             send(total.at[slot, lower], recv_by.at[at], send_by_sem, recv_by_sem.at[at],
-                 z, column(lax.rem(y + dy, ny), x, c))
+                 z, column(remainder(y + dy, ny), x, c))
 
     def after_first(step):
         dx, dy, dz = offsets_at(step)
@@ -262,13 +278,13 @@
         def _():
             at = (dy - 1) * nz + dz
             send(total.at[slot, upper], recv_ay.at[at], send_ay_sem, recv_ay_sem.at[at],
-                 z, column(lax.rem(y + dy, ny), x, c))
+                 z, column(remainder(y + dy, ny), x, c))
 
         @pl.when(jnp.logical_and(dy == 0, dx > 0))
         def _():
             at = (dx - 1) * nz + dz
             send(total.at[slot, lower], recv_bx.at[at], send_bx_sem, recv_bx_sem.at[at],
-                 z, column(y, lax.rem(x + dx, nx), c))
+                 z, column(y, remainder(x + dx, nx), c))
 
     def after_second(step):
         dx, dy, dz = offsets_at(step)
@@ -283,7 +299,7 @@
             @pl.when(dz > 0)
             def _():
                 send(total.at[dz], recv_z.at[dz - 1], send_z_sem, recv_z_sem.at[dz - 1],
-                     lax.rem(z + dz, nz), col)
+                     remainder(z + dz, nz), col)
 
     first_source = source_of(*offsets_at(0)) + 1 - c
     to_smem(first_source).wait()

time: 44.1 us -> 44.3 us (level)
  no operation moved by 1% of the time
where the time goes in v3:
time: 44.3 us; the launch traced here: 44.1 us
  Pallas kernels  42.5 us (96%)
  other arithmetic  1.6 us (4%)
    pallas_call x1, Pallas kernels, per_device(): pl.pallas_call(functools.partial(kernel, (nz, ncol, ny, nx, nc, cap)), ou...  42.5 us
    concatenate x1, other arithmetic, per_device(): return jnp.concatenate([pooled, dense_out], axis=1)  1.6 us

profile of v3, /device:TPU:0, one launch (start us, length us, event | category | flops | bytes accessed | tf_op | source)
XLA Modules:
  0.0 44.1 jit_solution(12195647671773594889)
XLA Ops:
  0.0 42.5 %shard_map.64 = (f32[128,128]{1,0:T(8,128)}, f32[128,256]{1,0:T(8,128)}) custom-call(f32[40960,128]{1,0:T(8,128)} %table_hbm.1, s32[50,128]{1,0:T(8,128)} %bitcast.3, s32[50,128]{1,0:T(8,128)} %bitcast.4, s32[1,128]{1,0:T(1,128)} %bitcast.5, bf16[128,256]{1,0:T(8,128)(2,1)} %dense_hbm.1, bf16[256,256]{1,0:T(8,128)(2,1)} %w_hbm.1), custom_call_target="tpu_custom_call" | custom-call | tf_op jit(solution)/shard_map/pallas_call | solution.py:355
  42.5 1.6 %pad_maximum_fusion = f32[128,384]{1,0:T(8,128)} fusion(f32[128,256]{1,0:T(8,128)} %get-tuple-element.8, f32[128,128]{1,0:T(8,128)} %get-tuple-element.7), kind=kLoop, calls=%fused_computation | loop fusion | flops 49152 | bytes 393216 | tf_op jit(solution)/shard_map/concatenate | solution.py:392
